TPU v7x, 256 devices: a whole 4x4x8 slice. The times are simulated.
256 devices in a mesh: dp: 8 (over z_lo, y), ctx: 32 (over x, z_hi, core).
Axes of the slice: x: 4, y: 4, z: 8 (z_hi: 4, z_lo: 2; z = z_hi * 2 + z_lo), core: 2. Of those that a mesh axis runs over, the one named last changes fastest.
Arguments:
- queries: bfloat16 [8, 8192, 2048], P('dp', 'ctx'), may hold values from -40 to 40
- keys: bfloat16 [8, 8192, 2048], P('dp', 'ctx'), may hold values from -40 to 40
- values: bfloat16 [8, 8192, 2048], P('dp', 'ctx'), may hold values from -6 to 6
- out_grad: bfloat16 [8, 8192, 4096], P('dp', 'ctx'), may hold values from -6 to 6
- q_init: bfloat16 [64, 4096], replicated, may hold values from -0.09375 to 0.09375
- lengths: int32 [8], P('dp'), may hold values from 4096 to 8192, as said below
Outputs:
- p_hat: float32 [64, 2048], replicated
- q_new: float32 [64, 4096], replicated
Inputs may be any that keep to these rules, and one draw needn't show every extreme that they name: `lengths`: one stream in every draw is valid over all its frames.
All inputs are finite; a program needn't handle non-finite values.
Results may differ from a plain program's by a relative error of at most 0.008.
Values may be sent and summed in bfloat16 or wider, within the bound.
A program may use at most 128 MiB of HBM per device.

v0:
```python
import jax
import jax.numpy as jnp
from jax import lax
from jax.sharding import PartitionSpec as P

HEAD_DIM = 128
WINDOW = 2048


def passed_along(block, axis, distance):
    devices = range(lax.axis_size(axis))
    route = [(i - distance, i) for i in devices if i - distance in devices]
    return lax.ppermute(block, axis, route)


def local(queries, keys, values, out_grad, q_init, lengths):
    q_local = queries[0]
    frames = q_local.shape[0]
    width = q_local.shape[1]
    heads = width // HEAD_DIM
    reach = WINDOW // frames
    scale = 1.0 / HEAD_DIM**0.5
    position = lax.axis_index("ctx")
    q_pos = position * frames + jnp.arange(frames, dtype=jnp.int32)
    q_heads = q_local.reshape(frames, heads, HEAD_DIM)
    paired = jnp.stack([keys[0], values[0]])

    def absorb(state, piece, offset):
        top, total, summed = state
        k_heads = piece[0].reshape(frames, heads, HEAD_DIM)
        v_heads = piece[1].reshape(frames, heads, HEAD_DIM)
        k_pos = offset + jnp.arange(frames, dtype=jnp.int32)
        keep = (
            (k_pos[None, :] <= q_pos[:, None])
            & (k_pos[None, :] > q_pos[:, None] - WINDOW)
            & (k_pos[None, :] >= 0)
        )
        score = (
            jnp.einsum("qhe,khe->hqk", q_heads, k_heads, preferred_element_type=jnp.float32) * scale
        )
        score = jnp.where(keep[None], score, -1e30)
        new_top = jnp.maximum(top, jnp.max(score, axis=-1))
        factor = jnp.exp(top - new_top)
        expo = jnp.exp(score - new_top[:, :, None])
        total = total * factor + jnp.sum(expo, axis=-1)
        update = jnp.einsum(
            "hqk,khe->qhe", expo.astype(jnp.bfloat16), v_heads, preferred_element_type=jnp.float32
        )
        summed = summed * jnp.transpose(factor)[:, :, None] + update
        return (new_top, total, summed)

    state = (
        jnp.full((heads, frames), -1e30, jnp.float32),
        jnp.zeros((heads, frames), jnp.float32),
        jnp.zeros((frames, heads, HEAD_DIM), jnp.float32),
    )
    state = absorb(state, paired, position * frames)
    for step in range(1, reach + 1):
        piece = passed_along(paired, "ctx", step)
        state = absorb(state, piece, (position - step) * frames)
    top, total, summed = state
    result = summed / jnp.transpose(total)[:, :, None]
    result = jnp.where((q_pos < lengths[0])[:, None, None], result, 0.0)
    attended = result.reshape(frames, width).astype(jnp.bfloat16)
    grad_local = out_grad[0]
    proj = jnp.dot(grad_local, jnp.transpose(q_init), preferred_element_type=jnp.float32).astype(
        jnp.bfloat16
    )
    p_term = jnp.dot(jnp.transpose(proj), attended, preferred_element_type=jnp.float32)
    p_sum = lax.psum(p_term, ("dp", "ctx"))
    gram = jnp.dot(
        p_sum,
        jnp.transpose(p_sum),
        precision=lax.Precision.HIGHEST,
        preferred_element_type=jnp.float32,
    )
    lower = jnp.linalg.cholesky(gram)
    p_hat = width**0.5 * lax.linalg.triangular_solve(lower, p_sum, left_side=True, lower=True)
    mapped = jnp.dot(
        attended, jnp.transpose(p_hat.astype(jnp.bfloat16)), preferred_element_type=jnp.float32
    ).astype(jnp.bfloat16)
    q_term = jnp.dot(jnp.transpose(mapped), grad_local, preferred_element_type=jnp.float32)
    all_frames = lax.axis_size("dp") * lax.axis_size("ctx") * frames
    q_new = lax.psum(q_term, ("dp", "ctx")) / all_frames**0.5
    return (p_hat, q_new)


def solution(mesh):
    placed = (
        P("dp", "ctx", None),
        P("dp", "ctx", None),
        P("dp", "ctx", None),
        P("dp", "ctx", None),
        P(),
        P("dp"),
    )
    return jax.shard_map(local, mesh=mesh, in_specs=placed, out_specs=(P(), P()), check_vma=False)
```

profile of v0, /device:TPU:1, one launch (start us, length us, event | category | flops | bytes accessed | tf_op | source)
XLA Modules:
  0.0 1015.2 jit_solution(11152242430755506321)
XLA Ops:
  7.2 1.6 copy.87
  8.9 2.3 copy.43
  11.1 2.8 pad_maximum_fusion
  13.9 5.2 collective-permute-start.7
  19.1 9.2 collective-permute-start.5
  28.3 4.0 collective-permute-start.4
  32.3 2.6 collective-permute-start.3
  34.9 5.9 collective-permute-start.2
  41.5 1.4 copy.88
  42.9 1.4 copy.89
  44.5 1.0 and_and_fusion.8
  45.5 1.0 fusion
  46.5 39.9 %collective-permute-done.7 = bf16[2,256,2048]{1,2,0:T(8,128)(2,1)} collective-permute-done((bf16[2,256,2048]{1,2,0:T(8,128)(2,1)}, bf16[2,256,2048]{1,2,0:T(8,128)(2,1)}, u32[]{:S(2)}, u32[]{:S(2)}) %collective-permute-start.7) | collective-permute-done | bytes 2097184 | tf_op jit(solution)/shard_map/ppermute | solution.py:13
  86.4 132.3 %collective-permute-start.1 = (bf16[2,256,2048]{1,2,0:T(8,128)(2,1)}, bf16[2,256,2048]{1,2,0:T(8,128)(2,1)S(1)}, u32[]{:S(2)}, u32[]{:S(2)}) collective-permute-start(bf16[2,256,2048]{1,2,0:T(8,128)(2,1)} %pad_maximum_fusion), channel_id=1, source_target_pairs={{0,2},{1,3},{2,4},{3,5},{4,6},{5,7},{6,8},{7,9},{8,10},{9,11},{10,... | collective-permute-start | bytes 6291464 | tf_op jit(solution)/shard_map/ppermute | solution.py:13
  218.7 2.7 fusion.165
  221.4 1.0 fusion.26
  222.5 3.2 collective-permute-start
  225.7 1.7 fusion.171
  227.4 1.0 fusion.24
  228.4 136.5 %collective-permute-done.4 = bf16[2,256,2048]{1,2,0:T(8,128)(2,1)} collective-permute-done((bf16[2,256,2048]{1,2,0:T(8,128)(2,1)}, bf16[2,256,2048]{1,2,0:T(8,128)(2,1)}, u32[]{:S(2)}, u32[]{:S(2)}) %collective-permute-start.4) | collective-permute-done | bytes 2097184 | tf_op jit(solution)/shard_map/ppermute | solution.py:13
  364.9 3.0 collective-permute-start.6
  367.9 2.7 fusion.170
  370.6 1.0 fusion.23
  371.6 2.6 fusion.169
  374.3 1.0 fusion.22
  375.3 2.7 fusion.168
  378.0 1.0 fusion.21
  379.1 1.2 fusion.167
  380.2 1.0 fusion.20
  381.2 52.4 %collective-permute-done = bf16[2,256,2048]{1,2,0:T(8,128)(2,1)S(1)} collective-permute-done((bf16[2,256,2048]{1,2,0:T(8,128)(2,1)}, bf16[2,256,2048]{1,2,0:T(8,128)(2,1)S(1)}, u32[]{:S(2)}, u32[]{:S(2)}) %collective-permute-start) | collective-permute-done | bytes 2097184 | tf_op jit(solution)/shard_map/ppermute | solution.py:13
  433.7 1.1 fusion.166
  434.8 1.0 fusion.19
  435.8 9.8 collective-permute-done.6
  445.6 3.0 fusion.172
  448.6 2.2 fusion.25
  450.9 0.9 fusion.1
  451.8 3.7 fusion.43
  455.4 0.9 fusion.3
  456.7 1.1 fusion.41
  457.8 1.1 fusion.17
  458.9 1.1 fusion.27
  460.0 0.9 fusion.5
  460.9 1.1 fusion.39
  462.0 0.9 fusion.7
  462.9 1.1 fusion.37
  464.1 0.9 fusion.9
  465.0 1.1 fusion.35
  466.1 0.9 fusion.11
  467.0 2.4 fusion.33
  469.5 0.9 fusion.13
  470.4 1.1 fusion.31
  471.5 0.9 fusion.15
  473.7 2.9 fusion.48
  476.6 3.4 fusion.102
  480.1 251.0 %all-reduce.3.cloned.1.call-done = f32[64,2048]{1,0:T(8,128)} async-done(((f32[64,2048]{1,0:T(8,128)}), f32[64,2048]{1,0:T(8,128)}) %all-reduce.3.cloned.1.call-update) | async-done | bytes 524304 | tf_op jit(solution)/shard_map/psum | solution.py:70
  731.1 1.8 fusion.173
  733.0 5.8 cholesky.16
  738.9 0.6 compare_reduce_fusion
  739.5 0.7 fusion.125
  740.2 4.9 custom-call.6
  745.1 2.5 convolution_multiply_fusion
  747.5 3.5 fusion.57
  751.0 254.8 %all-reduce.5.cloned.1.call-done = f32[64,4096]{1,0:T(8,128)} async-done(((f32[64,4096]{1,0:T(8,128)}), f32[64,4096]{1,0:T(8,128)}) %all-reduce.5.cloned.1.call-update) | async-done | bytes 1048592 | tf_op jit(solution)/shard_map/psum | solution.py:84
  1005.9 2.3 broadcast_multiply_fusion
  (42 shorter events, 2.0 us)
Async XLA Ops:
  7.2 469.4 %copy-start = (bf16[1,256,4096]{2,1,0:T(8,128)(2,1)S(1)}, bf16[1,256,4096]{2,1,0:T(8,128)(2,1)}, u32[]{:S(2)}) copy-start(bf16[1,256,4096]{2,1,0:T(8,128)(2,1)} %param.9) | copy-start | bytes 6291460
  7.2 723.9 %all-reduce.3.cloned.1.call-start = ((), (), s32[]{:S(2)}) async-start(), calls=%async_computation | async-start | bytes 1048576 | tf_op jit(solution)/shard_map/psum | solution.py:70
  13.9 72.5 %collective-permute-start.7 = (bf16[2,256,2048]{1,2,0:T(8,128)(2,1)}, bf16[2,256,2048]{1,2,0:T(8,128)(2,1)}, u32[]{:S(2)}, u32[]{:S(2)}) collective-permute-start(bf16[2,256,2048]{1,2,0:T(8,128)(2,1)} %pad_maximum_fusion), channel_id=1, source_target_pairs={{0,8},{1,9},{2,10},{3,11},{4,12},{5,13},{6,14},{7,15},{8,16},{9,17... | collective-permute-start | bytes 6291464 | tf_op jit(solution)/shard_map/ppermute | solution.py:13
  19.1 203.4 %collective-permute-start.5 = (bf16[2,256,2048]{1,2,0:T(8,128)(2,1)}, bf16[2,256,2048]{1,2,0:T(8,128)(2,1)}, u32[]{:S(2)}, u32[]{:S(2)}) collective-permute-start(bf16[2,256,2048]{1,2,0:T(8,128)(2,1)} %pad_maximum_fusion), channel_id=1, source_target_pairs={{0,6},{1,7},{2,8},{3,9},{4,10},{5,11},{6,12},{7,13},{8,14},{9,15},... | collective-permute-start | bytes 6291464 | tf_op jit(solution)/shard_map/ppermute | solution.py:13
  28.3 336.6 %collective-permute-start.4 = (bf16[2,256,2048]{1,2,0:T(8,128)(2,1)}, bf16[2,256,2048]{1,2,0:T(8,128)(2,1)}, u32[]{:S(2)}, u32[]{:S(2)}) collective-permute-start(bf16[2,256,2048]{1,2,0:T(8,128)(2,1)} %pad_maximum_fusion), channel_id=1, source_target_pairs={{0,5},{1,6},{2,7},{3,8},{4,9},{5,10},{6,11},{7,12},{8,13},{9,14},{... | collective-permute-start | bytes 6291464 | tf_op jit(solution)/shard_map/ppermute | solution.py:13
  32.3 339.3 %collective-permute-start.3 = (bf16[2,256,2048]{1,2,0:T(8,128)(2,1)}, bf16[2,256,2048]{1,2,0:T(8,128)(2,1)}, u32[]{:S(2)}, u32[]{:S(2)}) collective-permute-start(bf16[2,256,2048]{1,2,0:T(8,128)(2,1)} %pad_maximum_fusion), channel_id=1, source_target_pairs={{0,4},{1,5},{2,6},{3,7},{4,8},{5,9},{6,10},{7,11},{8,12},{9,13},{1... | collective-permute-start | bytes 6291464 | tf_op jit(solution)/shard_map/ppermute | solution.py:13
  34.9 340.4 %collective-permute-start.2 = (bf16[2,256,2048]{1,2,0:T(8,128)(2,1)}, bf16[2,256,2048]{1,2,0:T(8,128)(2,1)}, u32[]{:S(2)}, u32[]{:S(2)}) collective-permute-start(bf16[2,256,2048]{1,2,0:T(8,128)(2,1)} %pad_maximum_fusion), channel_id=1, source_target_pairs={{0,3},{1,4},{2,5},{3,6},{4,7},{5,8},{6,9},{7,10},{8,11},{9,12},{10... | collective-permute-start | bytes 6291464 | tf_op jit(solution)/shard_map/ppermute | solution.py:13
  86.4 292.7 %collective-permute-start.1 = (bf16[2,256,2048]{1,2,0:T(8,128)(2,1)}, bf16[2,256,2048]{1,2,0:T(8,128)(2,1)S(1)}, u32[]{:S(2)}, u32[]{:S(2)}) collective-permute-start(bf16[2,256,2048]{1,2,0:T(8,128)(2,1)} %pad_maximum_fusion), channel_id=1, source_target_pairs={{0,2},{1,3},{2,4},{3,5},{4,6},{5,7},{6,8},{7,9},{8,10},{9,11},{10,... | collective-permute-start | bytes 6291464 | tf_op jit(solution)/shard_map/ppermute | solution.py:13
  222.5 211.2 %collective-permute-start = (bf16[2,256,2048]{1,2,0:T(8,128)(2,1)}, bf16[2,256,2048]{1,2,0:T(8,128)(2,1)S(1)}, u32[]{:S(2)}, u32[]{:S(2)}) collective-permute-start(bf16[2,256,2048]{1,2,0:T(8,128)(2,1)} %pad_maximum_fusion), channel_id=1, source_target_pairs={{0,1},{1,2},{2,3},{3,4},{4,5},{5,6},{6,7},{7,8},{8,9},{9,10},{10,1... | collective-permute-start | bytes 6291464 | tf_op jit(solution)/shard_map/ppermute | solution.py:13
  364.9 80.7 %collective-permute-start.6 = (bf16[2,256,2048]{1,2,0:T(8,128)(2,1)}, bf16[2,256,2048]{1,2,0:T(8,128)(2,1)}, u32[]{:S(2)}, u32[]{:S(2)}) collective-permute-start(bf16[2,256,2048]{1,2,0:T(8,128)(2,1)} %pad_maximum_fusion), channel_id=1, source_target_pairs={{0,7},{1,8},{2,9},{3,10},{4,11},{5,12},{6,13},{7,14},{8,15},{9,16}... | collective-permute-start | bytes 6291464 | tf_op jit(solution)/shard_map/ppermute | solution.py:13
  455.4 1.2 copy-start.5
  458.8 2.1 copy-start.3
  460.9 2.0 copy-start.2
  462.9 2.0 copy-start.1
  467.0 3.3 copy-start.4
  470.4 2.1 copy-start.8
  471.5 1.6 copy-start.6
  471.5 2.2 copy-start.7
  480.1 525.8 %all-reduce.5.cloned.1.call-start = ((), (), s32[]{:S(2)}) async-start(), calls=%async_computation.1 | async-start | bytes 2097152 | tf_op jit(solution)/shard_map/psum | solution.py:84
Sparse Core Ops, SparseCore 0:
  480.2 250.8 all-reduce.2
  751.1 254.6 all-reduce.4
where the time goes:
time: 1020 us
  waiting for transfers between devices  744 us (73%)
  starting transfers between devices  166 us (16%)
  matrix products  37.3 us (4%)
  other arithmetic  26.4 us (3%)
  local copies, waits for them, and re-layouts  26.1 us (3%)
  between operations  15.4 us (2%)
    psum x1, waiting for transfers between devices, local(): q_new = lax.psum(q_term, ('dp', 'ctx')) / all_frames ** 0.5  255 us
    psum x1, waiting for transfers between devices, local(): p_sum = lax.psum(p_term, ('dp', 'ctx'))  251 us
    ppermute x8, waiting for transfers between devices, passed_along(): return lax.ppermute(block, axis, route)  239 us
    ppermute x8, starting transfers between devices, passed_along(): return lax.ppermute(block, axis, route)  165 us
  transfers between devices with their start and end apart: 10, of which 6 were waited for; matrix products, arithmetic and copies ran while one was open for 3% of the time, Pallas kernels for 0%

commit v1 on v0

v1 whole, which is shorter than its diff:
```python
import functools

import jax
import jax.numpy as jnp
from jax import lax
from jax.experimental import pallas as pl
from jax.experimental.pallas import tpu as pltpu
from jax.sharding import PartitionSpec as P

HD = 128
FR = 256
HEADS = 16
WIDTH = HEADS * HD
D = 4096
RANK = 64
REACH = 8
GROUPS = 4
PER = HEADS // GROUPS
CH = PER * HD
HALF = CH // 2
LOG2E = 1.4426950408889634
SCALE2 = LOG2E / HD**0.5
LOW = -1e30
MESH = pl.DeviceIdType.MESH
F32 = jnp.float32
BF16 = jnp.bfloat16


def nt(a, b, **kw):
    return lax.dot_general(a, b, (((1,), (1,)), ((), ())), preferred_element_type=F32, **kw)


def nn(a, b, **kw):
    return lax.dot_general(a, b, (((1,), (0,)), ((), ())), preferred_element_type=F32, **kw)


def kernel(
    len_ref, q_ref, k_ref, v_ref, g_ref, qi_ref, phat_ref, qnew_ref,
    qbuf, ebuf, st_out, st_in, f_out, f_in, pj_in, mp_out, mp_in,
    xp, xp_c, xp_xy, xp_z, psum, xq, xq_c, xq_xy, xq_z, qt,
    ss_x, ss_dm, ss_dp, ss_f1, ss_f3, ss_t, ss_sib, rs_slot, rs_h, rs_sib,
    ss_st, rs_st, ss_f, rs_f, ss_p, rs_p, ss_m, rs_m,
    ss_c, rs_c, ss_xy, rs_xy, ss_z, rs_z, ss_ag, rs_ag,
):
    dp = lax.axis_index("dp")
    ctx = lax.axis_index("ctx")
    zlo, y = dp // 4, dp % 4
    x, zh, core = ctx // 8, (ctx // 2) % 4, ctx % 2
    plane = x * 4 + y
    zz = zh * 2 + zlo

    def at_ctx(i):
        return (dp, lax.rem(i + 64, 32))

    def at_plane(p):
        return (zlo * 4 + p % 4, (p // 4) * 8 + zh * 2 + core)

    def at_z(z):
        return ((z % 2) * 4 + y, x * 8 + (z // 2) * 2 + core)

    sibling = (dp, ctx + 1 - 2 * core)
    up = (dp, x * 8 + ((zh + 1) % 4) * 2 + core)
    down = (dp, x * 8 + ((zh + 3) % 4) * 2 + core)
    left = at_ctx(ctx - 8)
    right = at_ctx(ctx + 8)

    def rc(src, dst, ss, rs, device):
        return pltpu.make_async_remote_copy(
            src_ref=src, dst_ref=dst, send_sem=ss, recv_sem=rs, device_id=device, device_id_type=MESH
        )

    bar = pltpu.get_barrier_semaphore()

    def greet_ctx(i, c):
        pl.semaphore_signal(bar, 1, device_id=at_ctx(ctx + i + 1), device_id_type=MESH)
        pl.semaphore_signal(bar, 1, device_id=at_ctx(ctx - i - 1), device_id_type=MESH)
        return c

    lax.fori_loop(0, REACH, greet_ctx, 0)

    def greet_plane(i, c):
        pl.semaphore_signal(bar, 1, device_id=at_plane((plane + i) % 16), device_id_type=MESH)
        return c

    lax.fori_loop(1, 16, greet_plane, 0)

    def greet_z(i, c):
        pl.semaphore_signal(bar, 1, device_id=at_z((zz + i) % 8), device_id_type=MESH)
        return c

    lax.fori_loop(1, 8, greet_z, 0)
    pl.semaphore_wait(bar, 2 * REACH + 15 + 7)

    def cols(g):
        return pl.ds(g * CH, CH)

    def chunk(d, g):
        return qbuf.at[d, :, cols(g)]

    mid = (zh == 1) | (zh == 2)
    part = jnp.where(mid, 0, HALF)

    def half(d, g):
        return qbuf.at[d, :, pl.ds(pl.multiple_of(g * CH + part, HALF), HALF)]

    def c_x(g):
        return rc(q_ref.at[:, cols(g)], chunk(8, g), ss_x.at[g], rs_slot.at[2, g], left)

    def c_dm(g, own):
        src = q_ref.at[:, cols(g)] if own else chunk(8, g)
        return rc(src, chunk(2, g), ss_dm.at[g], rs_slot.at[0, g], down)

    def c_dp(g, own):
        src = q_ref.at[:, cols(g)] if own else chunk(8, g)
        return rc(src, chunk(6, g), ss_dp.at[g], rs_slot.at[1, g], up)

    def c_f1(g):
        slot = jnp.where(zh == 0, 0, 4)
        sem = jnp.where(mid, 0, jnp.where(zh == 0, 2, 1))
        return rc(half(2, g), half(slot, g), ss_f1.at[g], rs_h.at[sem, g], down)

    def c_f3(g):
        slot = jnp.where(zh == 3, 0, 4)
        sem = jnp.where(mid, 0, jnp.where(zh == 3, 2, 1))
        return rc(half(6, g), half(slot, g), ss_f3.at[g], rs_h.at[sem, g], up)

    def beta(d, g):
        return qbuf.at[d, :, pl.ds(g * CH + HALF, HALF)]

    def alpha(d, g):
        return qbuf.at[d, :, pl.ds(g * CH, HALF)]

    def c_t(g):
        far = (dp, lax.rem(ctx + jnp.where(zh == 0, 8, 24), 32))
        return rc(beta(0, g), beta(4, g), ss_t.at[g], rs_h.at[1, g], far)

    def c_sib(k, g):
        if k == 0:
            src, to = q_ref.at[:, cols(g)], 1
        elif k == 4:
            src, to = chunk(8, g), 7
        else:
            src, to = chunk(2 * k, g), 2 * k - 1 + 2 * core
        return rc(src, chunk(to, g), ss_sib.at[k, g], rs_sib.at[(to - 1) // 2, g], sibling)

    def got(dst, rs):
        rc(dst, dst, ss_x.at[0], rs, sibling).wait_recv()

    keep_row = lax.broadcasted_iota(jnp.int32, (FR, FR), 0)
    keep_col = lax.broadcasted_iota(jnp.int32, (FR, FR), 1)

    def unit(src, d, h, mask):
        hs = pl.ds(pl.multiple_of(h * HD, HD), HD)
        qh = q_ref[:, hs] if src is None else qbuf[src, :, hs]
        s = nt(k_ref[:, hs], qh)
        if mask == 0:
            s = jnp.where(keep_row <= keep_col, s, LOW)
        elif mask == 8:
            s = jnp.where(keep_row > keep_col, s, LOW)
        m = jnp.max(s, axis=0, keepdims=True)
        e = jnp.exp2((s - m) * SCALE2)
        ebuf[d * HEADS + h] = e.astype(BF16)
        row = (d * GROUPS + h // PER) * 8 + h % PER
        st_out[pl.ds(row, 1), :] = m
        st_out[pl.ds(row + PER, 1), :] = jnp.sum(e, axis=0, keepdims=True)

    def units(first, count, g):
        def body(i, c):
            d = first + 2 * (i // PER)
            unit(d, d, g * PER + i % PER, None)
            return c

        lax.fori_loop(0, count * PER, body, 0)

    def units_edge(d, lo, hi):
        def body(h, c):
            unit(None if d == 0 else 8, d, h, d)
            return c

        lax.fori_loop(lo, hi, body, 0)

    def on_x(g):
        got(chunk(8, g), rs_slot.at[2, g])

        @pl.when(zh < 3)
        def _():
            c_dp(g, False).start()

        @pl.when(zh == 0)
        def _():
            c_dm(g, False).start()

        @pl.when(core == 0)
        def _():
            c_sib(4, g).start()

    def on_1(g):
        got(chunk(2, g), rs_slot.at[0, g])
        c_f1(g).start()
        c_sib(1, g).start()

    def on_3(g):
        got(chunk(6, g), rs_slot.at[1, g])
        c_f3(g).start()
        c_sib(3, g).start()

    def on_2(g):
        @pl.when((zh == 0) | (zh == 3))
        def _():
            got(beta(0, g), rs_h.at[2, g])
            c_t(g).start()

        got(alpha(4, g), rs_h.at[0, g])
        got(beta(4, g), rs_h.at[1, g])
        c_sib(2, g).start()

    def on_sib(g):
        for k in range(4):
            got(chunk(2 * k + 1, g), rs_sib.at[k, g])

    def st_rows(ref, d, g):
        return ref.at[pl.ds(pl.multiple_of((d * GROUPS + g) * 8, 8), 8), :]

    def c_st(d, g):
        i = d * GROUPS + g
        return rc(st_rows(st_out, d, g), st_rows(st_in, d, g), ss_st.at[i], rs_st.at[i], at_ctx(ctx + d))

    def c_f(d, g):
        i = d * GROUPS + g
        return rc(st_rows(f_out, d, g), st_rows(f_in, d, g), ss_f.at[i], rs_f.at[i], at_ctx(ctx - d))

    def c_p(d):
        return rc(pj_in.at[0], pj_in.at[d], ss_p.at[d], rs_p.at[d], at_ctx(ctx - d))

    def c_m(d):
        return rc(mp_out.at[d], mp_in.at[d], ss_m.at[d], rs_m.at[d], at_ctx(ctx + d))

    def each(lo, hi, do):
        def body(i, c):
            do(i)
            return c

        lax.fori_loop(lo, hi, body, 0)

    def send_stats(g):
        each(1, REACH + 1, lambda d: c_st(d, g).start())

    def make_factors(g):
        each(1, REACH + 1, lambda d: c_st(d, g).wait_recv())
        tops, sums = [], []
        for d in range(REACH + 1):
            rows = (st_out if d == 0 else st_in)[pl.ds((d * GROUPS + g) * 8, 8), :]
            there = ctx >= d
            tops.append(jnp.where(there, rows[:PER], LOW))
            sums.append(jnp.where(there, rows[PER:], 0.0))
        top = functools.reduce(jnp.maximum, tops)
        ws = [jnp.exp2((t - top) * SCALE2) for t in tops]
        total = functools.reduce(jnp.add, [w * s for w, s in zip(ws, sums)])
        pos = ctx * FR + lax.broadcasted_iota(jnp.int32, (PER, FR), 1)
        inv = jnp.where(pos < len_ref[0], 1.0 / total, 0.0)
        for d in range(REACH + 1):
            f = jnp.where(ctx >= d, ws[d] * inv, 0.0)
            (f_in if d == 0 else f_out)[pl.ds((d * GROUPS + g) * 8, 8), :] = jnp.concatenate([f, f], axis=0)
        each(1, REACH + 1, lambda d: c_f(d, g).start())

    def p_heads(g):
        each(1, REACH + 1, lambda d: c_f(d, g).wait_recv())

        def body(i, c):
            h = g * PER + i
            hs = pl.ds(pl.multiple_of(h * HD, HD), HD)
            acc = jnp.zeros((RANK, FR), F32)
            for d in range(REACH + 1):
                f = f_in[pl.ds((d * GROUPS + g) * 8 + i, 1), :]
                pf = (pj_in[d].astype(F32) * f).astype(BF16)
                acc = acc + nt(pf, ebuf[d * HEADS + h])
            xp[:, hs] = nn(acc.astype(BF16), v_ref[:, hs])
            return c

        lax.fori_loop(0, PER, body, 0)

    def reduce_all(a, buf, buf_c, buf_xy, buf_z, out, rows, width, z_split, scale):
        half_w = width // 2
        mine = pl.ds(pl.multiple_of(core * half_w, half_w), half_w)
        other = pl.ds(pl.multiple_of((1 - core) * half_w, half_w), half_w)
        per_col = RANK // rows
        cc = rc(buf.at[:, other], buf_c, ss_c.at[2 * a], rs_c.at[2 * a], sibling)
        cc.start()
        cc.wait_recv()

        def add(i, c):
            s = pl.ds(pl.multiple_of(i * 128, 128), 128)
            t = pl.ds(pl.multiple_of(core * half_w + i * 128, 128), 128)
            buf_c[:, s] = buf_c[:, s] + buf[:, t]
            return c

        lax.fori_loop(0, half_w // 128, add, 0)

        def piece(ref, p, base):
            r = pl.ds(pl.multiple_of((p % per_col) * rows, rows), rows)
            c = pl.ds(pl.multiple_of(base + (p // per_col) * 128, 128), 128)
            return ref.at[r, c]

        def c_xy(k):
            p = (plane + k) % 16
            return rc(piece(buf_c, p, 0), buf_xy.at[plane], ss_xy.at[a, k], rs_xy.at[a, plane], at_plane(p))

        def got_xy(k):
            p = (plane + k) % 16
            got(buf_xy.at[p], rs_xy.at[a, p])

        each(1, 16, lambda k: c_xy(k).start())
        buf_xy[plane] = piece(buf_c, plane, 0)[...]
        each(1, 16, got_xy)
        part_sum = buf_xy[0]
        for p in range(1, 16):
            part_sum = part_sum + buf_xy[p]
        if z_split:
            buf_xy[0] = part_sum
            zr = rows // 8

            def c_z(k):
                z = (zz + k) % 8
                src = buf_xy.at[0, pl.ds(pl.multiple_of(z * zr, zr), zr), :]
                return rc(src, buf_z.at[zz], ss_z.at[a, k], rs_z.at[a, zz], at_z(z))

            def got_z(k):
                z = (zz + k) % 8
                got(buf_z.at[z], rs_z.at[a, z])

            each(1, 8, lambda k: c_z(k).start())
            buf_z[zz] = buf_xy[0, pl.ds(pl.multiple_of(zz * zr, zr), zr), :]
            each(1, 8, got_z)
            total = buf_z[0]
            for z in range(1, 8):
                total = total + buf_z[z]
            home = piece(out, plane, core * half_w)
            r0 = (plane % per_col) * rows
            c0 = pl.ds(pl.multiple_of(core * half_w + (plane // per_col) * 128, 128), 128)

            def line(z):
                return out.at[pl.ds(pl.multiple_of(r0 + z * zr, zr), zr), c0]

            out[pl.ds(pl.multiple_of(r0 + zz * zr, zr), zr), c0] = total * scale

            def c_z2(k):
                return rc(line(zz), line(zz), ss_z.at[2, k], rs_z.at[2, zz], at_z((zz + k) % 8))

            each(1, 8, lambda k: c_z2(k).start())

            def got_z2(k):
                z = (zz + k) % 8
                got(line(z), rs_z.at[2, z])

            each(1, 8, got_z2)
        else:
            buf_z[zz] = part_sum

            def c_z(k):
                return rc(buf_z.at[zz], buf_z.at[zz], ss_z.at[a, k], rs_z.at[a, zz], at_z((zz + k) % 8))

            each(1, 8, lambda k: c_z(k).start())

            def got_z(k):
                z = (zz + k) % 8
                got(buf_z.at[z], rs_z.at[a, z])

            each(1, 8, got_z)
            total = buf_z[0]
            for z in range(1, 8):
                total = total + buf_z[z]
            r0 = pl.ds(pl.multiple_of((plane % per_col) * rows, rows), rows)
            c0 = pl.ds(pl.multiple_of(core * half_w + (plane // per_col) * 128, 128), 128)
            out[r0, c0] = total * scale

        def c_ag(k):
            ref = piece(out, plane, core * half_w)
            return rc(ref, ref, ss_ag.at[a, k], rs_ag.at[a, plane], at_plane((plane + k) % 16))

        def got_ag(k):
            p = (plane + k) % 16
            got(piece(out, p, core * half_w), rs_ag.at[a, p])

        each(1, 16, lambda k: c_ag(k).start())
        each(1, 16, got_ag)
        c2 = rc(out.at[:, mine], out.at[:, mine], ss_c.at[2 * a + 1], rs_c.at[2 * a + 1], sibling)
        c2.start()
        got(out.at[:, other], rs_c.at[2 * a + 1])
        cc.wait_send()
        c2.wait_send()
        each(1, 16, lambda k: c_xy(k).wait_send())
        each(1, 16, lambda k: c_ag(k).wait_send())
        each(1, 8, lambda k: c_z(k).wait_send())
        if z_split:
            each(1, 8, lambda k: c_z2(k).wait_send())

    for g in range(GROUPS):
        c_x(g).start()

        @pl.when(zh > 0)
        def _():
            c_dm(g, True).start()

        @pl.when(zh == 3)
        def _():
            c_dp(g, True).start()

        @pl.when(core == 1)
        def _():
            c_sib(0, g).start()

    pj_in[0] = nt(qi_ref[...], g_ref[...]).astype(BF16)
    each(1, REACH + 1, lambda d: c_p(d).start())
    units_edge(0, 0, HEADS)
    on_x(0)
    on_x(1)
    on_1(0)
    on_x(2)
    on_3(0)
    on_x(3)
    units_edge(8, 0, HEADS)
    units(2, 1, 0)
    units(6, 1, 0)
    for g in range(1, GROUPS):
        on_1(g)
        units(2, 1, g)
        on_3(g)
        units(6, 1, g)
        on_2(g - 1)
        on_sib(g - 1)
        units(1, 4, g - 1)
        units(4, 1, g - 1)
        send_stats(g - 1)
        if g > 1:
            make_factors(g - 2)
        if g == 2:
            each(1, REACH + 1, lambda d: c_p(d).wait_recv())
        if g > 2:
            p_heads(g - 3)
    last = GROUPS - 1
    on_2(last)
    units(4, 1, last)
    on_sib(last)
    units(1, 4, last)
    send_stats(last)
    make_factors(last - 1)
    p_heads(last - 2)
    make_factors(last)
    p_heads(last - 1)
    p_heads(last)

    reduce_all(0, xp, xp_c, xp_xy, xp_z, psum, 32, WIDTH, False, 1.0)

    p_sum = psum[...]
    gram = nt(p_sum, p_sum, precision=lax.Precision.HIGHEST)
    row_i = lax.broadcasted_iota(jnp.int32, (RANK, 2 * RANK), 0)
    col_i = lax.broadcasted_iota(jnp.int32, (RANK, 2 * RANK), 1)
    a = jnp.concatenate([gram, jnp.zeros((RANK, RANK), F32)], axis=1)
    a = jnp.where(col_i == row_i + RANK, 1.0, a)
    pivots = jnp.zeros((RANK, 2 * RANK), F32)
    for k in range(RANK):
        wide = jnp.broadcast_to(a[:, k : k + 1], (RANK, 2 * RANK))
        piv = wide[k : k + 1, :]
        line = a[k : k + 1, :] / piv
        pivots = jnp.where(row_i == k, piv, pivots)
        a = a - jnp.where(row_i > k, wide, 0.0) * line
    inv_low = a[:, RANK:] * (lax.rsqrt(pivots[:, RANK:]) * (WIDTH**0.5))
    phat_ref[...] = nn(inv_low, p_sum, precision=lax.Precision.HIGHEST)

    def values_in(h, c):
        hs = pl.ds(pl.multiple_of(h * HD, HD), HD)
        pj_in[pl.ds(REACH + 1 + h, 1)] = nt(phat_ref[:, hs].astype(BF16), v_ref[:, hs]).astype(BF16)[None]
        return c

    lax.fori_loop(0, HEADS, values_in, 0)

    def mapped_of(i, c):
        d = REACH - i

        def head(h, acc):
            f = f_in[pl.ds((d * GROUPS + h // PER) * 8 + h % PER, 1), :]
            return acc + nn(pj_in[REACH + 1 + h], ebuf[d * HEADS + h]) * f

        acc = lax.fori_loop(0, HEADS, head, jnp.zeros((RANK, FR), F32))
        mp_out[pl.ds(d, 1)] = acc.astype(BF16)[None]

        @pl.when(d > 0)
        def _():
            c_m(d).start()

        return c

    lax.fori_loop(0, REACH + 1, mapped_of, 0)
    acc = mp_out[0].astype(F32)
    for d in range(1, REACH + 1):
        c_m(d).wait_recv()
        acc = acc + jnp.where(ctx >= d, mp_in[d].astype(F32), 0.0)
    mapped = acc.astype(BF16)

    def q_cols(i, c):
        s = pl.ds(pl.multiple_of(i * 512, 512), 512)
        xq[:, s] = nn(mapped, g_ref[:, s])
        return c

    lax.fori_loop(0, D // 512, q_cols, 0)
    reduce_all(1, xq, xq_c, xq_xy, xq_z, qt, RANK, D, True, 1.0 / 256.0)
    qnew_ref[...] = qt[...]

    for g in range(GROUPS):
        c_x(g).wait_send()
        c_dm(g, True).wait_send()
        c_dp(g, True).wait_send()
        c_f1(g).wait_send()
        c_f3(g).wait_send()
        for k in (1, 2, 3):
            c_sib(k, g).wait_send()

        @pl.when((zh == 0) | (zh == 3))
        def _():
            c_t(g).wait_send()

        @pl.when(core == 1)
        def _():
            c_sib(0, g).wait_send()

        @pl.when(core == 0)
        def _():
            c_sib(4, g).wait_send()

        each(1, REACH + 1, lambda d: c_st(d, g).wait_send())
        each(1, REACH + 1, lambda d: c_f(d, g).wait_send())
    each(1, REACH + 1, lambda d: c_p(d).wait_send())
    each(1, REACH + 1, lambda d: c_m(d).wait_send())


def local(queries, keys, values, out_grad, q_init, lengths):
    dma = pltpu.SemaphoreType.DMA
    n = REACH + 1
    vm = pl.BlockSpec(memory_space=pltpu.VMEM)
    p_hat, q_new = pl.pallas_call(
        kernel,
        out_shape=(
            jax.ShapeDtypeStruct((RANK, WIDTH), F32),
            jax.ShapeDtypeStruct((RANK, D), F32),
        ),
        in_specs=[pl.BlockSpec(memory_space=pltpu.SMEM)] + [vm] * 5,
        out_specs=(vm, vm),
        scratch_shapes=[
            pltpu.VMEM((n, FR, WIDTH), BF16),
            pltpu.VMEM((n * HEADS, FR, FR), BF16),
            pltpu.VMEM((n * GROUPS * 8, FR), F32),
            pltpu.VMEM((n * GROUPS * 8, FR), F32),
            pltpu.VMEM((n * GROUPS * 8, FR), F32),
            pltpu.VMEM((n * GROUPS * 8, FR), F32),
            pltpu.VMEM((n + HEADS, RANK, FR), BF16),
            pltpu.VMEM((n, RANK, FR), BF16),
            pltpu.VMEM((n, RANK, FR), BF16),
            pltpu.VMEM((RANK, WIDTH), F32),
            pltpu.VMEM((RANK, WIDTH // 2), F32),
            pltpu.VMEM((16, 32, 128), F32),
            pltpu.VMEM((8, 32, 128), F32),
            pltpu.VMEM((RANK, WIDTH), F32),
            pltpu.VMEM((RANK, D), F32),
            pltpu.VMEM((RANK, D // 2), F32),
            pltpu.VMEM((16, RANK, 128), F32),
            pltpu.VMEM((8, 8, 128), F32),
            pltpu.VMEM((RANK, D), F32),
            dma((4,)), dma((4,)), dma((4,)), dma((4,)), dma((4,)), dma((4,)), dma((5, 4)),
            dma((3, 4)), dma((3, 4)), dma((4, 4)),
            dma((n * GROUPS,)), dma((n * GROUPS,)), dma((n * GROUPS,)), dma((n * GROUPS,)),
            dma((n,)), dma((n,)), dma((n,)), dma((n,)),
            dma((4,)), dma((4,)), dma((2, 16)), dma((2, 16)), dma((3, 8)), dma((3, 8)),
            dma((2, 16)), dma((2, 16)),
        ],
        compiler_params=pltpu.CompilerParams(
            collective_id=0, has_side_effects=True, vmem_limit_bytes=60 << 20
        ),
        name="attend",
    )(lengths, queries[0], keys[0], values[0], out_grad[0], q_init)
    return (p_hat, q_new)


def solution(mesh):
    placed = (
        P("dp", "ctx", None),
        P("dp", "ctx", None),
        P("dp", "ctx", None),
        P("dp", "ctx", None),
        P(),
        P("dp"),
    )
    return jax.shard_map(local, mesh=mesh, in_specs=placed, out_specs=(P(), P()), check_vma=False)
```

time: 1020 us -> 237 us (0.23)
  waiting for transfers between devices: 744 us -> 0 us
  Pallas kernels: 0 us -> 231 us
  starting transfers between devices: 166 us -> 0 us
  matrix products: 37.3 us -> 0 us
  other arithmetic: 26.4 us -> 0 us
  local copies, waits for them, and re-layouts: 26.1 us -> 4.14 us
  between operations: 15.4 us -> 1.29 us
    psum x2 -> x0, waiting for transfers between devices: 506 us -> none  [the longest x1 255 us: local(): q_new = lax.psum(q_term, ('dp', 'ctx')) / all_frames ** 0.5]
    ppermute x8 -> x0, waiting for transfers between devices: 239 us -> none  [passed_along(): return lax.ppermute(block, axis, route)]
    pallas_call x0 -> x1, Pallas kernels: none -> 231 us  [local(): pl.pallas_call(kernel, out_shape=(jax.ShapeDtypeStruct((RANK, WIDTH), F32...]
    ppermute x8 -> x0, starting transfers between devices: 165 us -> none  [passed_along(): return lax.ppermute(block, axis, route)]
    dot_general x21 -> x0, matrix products: 34.8 us -> none  [the longest x9 15.7 us: absorb(): jnp.einsum('hqk,khe->qhe', expo.astype(jnp.bfloat16), v_heads, preferred_...]
    slice x8 -> x0, local copies, waits for them, and re-layouts: 17.7 us -> none  [the longest x7 14.7 us: absorb(): v_heads = piece[1].reshape(frames, heads, HEAD_DIM)]
    another operation x6 -> x0, other arithmetic: 14.8 us -> none  [the longest x3 6.52 us: local(): lower = jnp.linalg.cholesky(gram)]
  transfers between devices with their start and end apart: 10 -> 0, of which waited for: 6 -> 0; matrix products, arithmetic and copies ran while one was open for 3% -> 0% of each run, Pallas kernels for 0% -> 0%
where the time goes in v1:
time: 237 us
  Pallas kernels  231 us (97%)
  local copies, waits for them, and re-layouts  4.14 us (2%)
    pallas_call x1, Pallas kernels, local(): pl.pallas_call(kernel, out_shape=(jax.ShapeDtypeStruct((RANK, WIDTH), F32...  231 us

profile of v1, /device:TPU:1, one launch (start us, length us, event | category | flops | bytes accessed | tf_op | source)
XLA Modules:
  0.0 236.7 jit_solution(4996229875916248431)
XLA Ops:
  1.3 231.2 %attend.1 = (f32[64,2048]{1,0:T(8,128)}, f32[64,4096]{1,0:T(8,128)}) custom-call(s32[1]{0:T(128)S(6)} %copy.10.len_ref, bf16[256,2048]{1,0:T(8,128)(2,1)} %bitcast.5, bf16[256,2048]{1,0:T(8,128)(2,1)} %bitcast.6, bf16[256,2048]{1,0:T(8,128)(2,1)} %bitcast.7, bf16[256,4096]{1,0:T(8,128)(2,1)} %bitcast.4, bf16[64,4096]{1,0:T(8,128)(2,1)} %qi_ref.1), custom_call_target="tpu_custom_call" | custom-call | tf_op jit(solution)/shard_map/attend/pallas_call | solution.py:540
  232.5 1.9 copy.11
  234.4 2.3 copy.12

commit v2 on v0

v2 whole, which is shorter than its diff:
```python
import functools

import jax
import jax.numpy as jnp
from jax import lax
from jax.experimental import pallas as pl
from jax.experimental.pallas import tpu as pltpu
from jax.sharding import PartitionSpec as P

HD = 128
FR = 256
HEADS = 16
WIDTH = HEADS * HD
D = 4096
RANK = 64
REACH = 8
GROUPS = 4
PER = HEADS // GROUPS
PARTS = GROUPS
CH = WIDTH // PARTS
LOG2E = 1.4426950408889634
SCALE2 = LOG2E / HD**0.5
LOW = -1e30
MESH = pl.DeviceIdType.MESH
F32 = jnp.float32
BF16 = jnp.bfloat16


def nt(a, b, **kw):
    return lax.dot_general(a, b, (((1,), (1,)), ((), ())), preferred_element_type=F32, **kw)


def nn(a, b, **kw):
    return lax.dot_general(a, b, (((1,), (0,)), ((), ())), preferred_element_type=F32, **kw)


def kernel(
    len_ref, q_any, k_any, v_any, g_any, qi_any, phat_ref, qnew_ref,
    q_ref, k_ref, v_ref, g_ref, qi_ref,
    qbuf, ebuf, mx, lg_out, lg_in, ls_out, ls_in, fac, pj_in, yacc, mp_out, mp_in,
    xp, xr, xz, psum, xq, xq_c, xq_b, xq_xy, xq_z, qg,
    ss_in, ss_x, ss_dm, ss_dp, ss_f1, ss_f3, ss_t, ss_sib, rs_slot, rs_h, rs_sib,
    ss_g, rs_g, ss_o, rs_o, ss_q, rs_q,
):
    dp = lax.axis_index("dp")
    ctx = lax.axis_index("ctx")
    zlo, y = dp // 4, dp % 4
    x, zh, core = ctx // 8, (ctx // 2) % 4, ctx % 2
    plane = x * 4 + y
    zz = zh * 2 + zlo
    rank = plane * 2 + core

    def at_ctx(i):
        return (dp, lax.rem(i + 64, 32))

    def at_plane(p):
        return (zlo * 4 + p % 4, (p // 4) * 8 + zh * 2 + core)

    def at_rank(r):
        return (zlo * 4 + (r // 2) % 4, (r // 8) * 8 + zh * 2 + r % 2)

    def at_z(z):
        return ((z % 2) * 4 + y, x * 8 + (z // 2) * 2 + core)

    sibling = (dp, ctx + 1 - 2 * core)
    up = (dp, x * 8 + ((zh + 1) % 4) * 2 + core)
    down = (dp, x * 8 + ((zh + 3) % 4) * 2 + core)
    left = at_ctx(ctx - 8)

    def rc(src, dst, ss, rs, device):
        return pltpu.make_async_remote_copy(
            src_ref=src, dst_ref=dst, send_sem=ss, recv_sem=rs, device_id=device, device_id_type=MESH
        )

    def each(lo, hi, do):
        def body(i, c):
            do(i)
            return c

        lax.fori_loop(lo, hi, body, 0)

    loads = [
        pltpu.make_async_copy(a, b, ss_in.at[i])
        for i, (a, b) in enumerate(
            ((q_any, q_ref), (k_any, k_ref), (g_any, g_ref), (qi_any, qi_ref), (v_any, v_ref))
        )
    ]
    for load in loads:
        load.start()

    bar = pltpu.get_barrier_semaphore()

    def greet(device):
        pl.semaphore_signal(bar, 1, device_id=device, device_id_type=MESH)

    def greet_ctx(i):
        greet(at_ctx(ctx + i))
        greet(at_ctx(ctx - i))

    each(1, REACH + 1, greet_ctx)
    each(1, 32, lambda i: greet(at_rank((rank + i) % 32)))
    each(1, 8, lambda i: greet(at_z((zz + i) % 8)))
    pl.semaphore_wait(bar, 2 * REACH + 31 + 7)

    def cols(g):
        return pl.ds(g * CH, CH)

    def chunk(d, g):
        return qbuf.at[d, :, cols(g)]

    mid = (zh == 1) | (zh == 2)
    edge = (zh == 0) | (zh == 3)

    def c_x(g):
        return rc(q_ref.at[:, cols(g)], chunk(8, g), ss_x.at[g], rs_slot.at[2, g], left)

    def c_dm(g, own):
        src = q_ref.at[:, cols(g)] if own else chunk(8, g)
        return rc(src, chunk(2, g), ss_dm.at[g], rs_slot.at[0, g], down)

    def c_dp(g, own):
        src = q_ref.at[:, cols(g)] if own else chunk(8, g)
        return rc(src, chunk(6, g), ss_dp.at[g], rs_slot.at[1, g], up)

    def c_f1(g):
        slot, sem = jnp.where(zh == 0, 0, 4), jnp.where(zh == 0, 1, 0)
        return rc(chunk(2, g), chunk(slot, g), ss_f1.at[g], rs_h.at[sem, g], down)

    def c_f3(g):
        slot, sem = jnp.where(zh == 3, 0, 4), jnp.where(zh == 3, 1, 0)
        return rc(chunk(6, g), chunk(slot, g), ss_f3.at[g], rs_h.at[sem, g], up)

    def forwards(g):
        return edge if g < PARTS // 2 else mid

    def c_t(g):
        far = (dp, lax.rem(ctx + jnp.where(zh == 0, 8, 24), 32))
        return rc(chunk(0, g), chunk(4, g), ss_t.at[g], rs_h.at[0, g], far)

    def c_sib(k, g):
        if k == 0:
            src, to = q_ref.at[:, cols(g)], 1
        elif k == 4:
            src, to = chunk(8, g), 7
        else:
            src, to = chunk(2 * k, g), 2 * k - 1 + 2 * core
        return rc(src, chunk(to, g), ss_sib.at[k, g], rs_sib.at[(to - 1) // 2, g], sibling)

    def got(dst, rs):
        rc(dst, dst, ss_x.at[0], rs, sibling).wait_recv()

    def left_all(src, ss):
        rc(src, src, ss, rs_g.at[0, 0], sibling).wait_send()

    keep_row = lax.broadcasted_iota(jnp.int32, (FR, FR), 0)
    keep_col = lax.broadcasted_iota(jnp.int32, (FR, FR), 1)

    def fold(a):
        return jnp.concatenate([a[:, : FR // 2], a[:, FR // 2 :]], axis=0)

    def unfold(a):
        return jnp.concatenate([a[:PER], a[PER:]], axis=1)

    def stat(ref, d, g):
        return ref.at[pl.ds(pl.multiple_of((d * GROUPS + g) * 8, 8), 8), :]

    def unit(d, g):
        tops, sums = [], []
        for i in range(PER):
            h = g * PER + i
            hs = slice(h * HD, h * HD + HD)
            qh = q_ref[:, hs] if isinstance(d, int) and d == 0 else qbuf[d, :, hs]
            s = nt(k_ref[:, hs], qh)
            if isinstance(d, int) and d == 0:
                s = jnp.where(keep_row <= keep_col, s, LOW)
            elif isinstance(d, int) and d == 8:
                s = jnp.where(keep_row > keep_col, s, LOW)
            m = jnp.max(s, axis=0, keepdims=True)
            e = jnp.exp2((s - m) * SCALE2)
            ebuf[d * HEADS + h] = e.astype(BF16)
            tops.append(m)
            sums.append(jnp.sum(e, axis=0, keepdims=True))
        top = jnp.concatenate(tops, axis=0) * SCALE2
        logs = top + jnp.log2(jnp.concatenate(sums, axis=0))
        stat(mx, d, g)[...] = jnp.concatenate([top, top], axis=0)
        lg_out[g, d] = fold(logs)

    def odd_units(g):
        each(0, 4, lambda i: unit(1 + 2 * i, g))

    def on_x(g):
        got(chunk(8, g), rs_slot.at[2, g])

        @pl.when(core == 0)
        def _():
            c_sib(4, g).start()

    def on_1(g):
        got(chunk(2, g), rs_slot.at[0, g])
        pl.when(forwards(g))(lambda: c_f1(g).start())
        c_sib(1, g).start()

    def on_3(g):
        got(chunk(6, g), rs_slot.at[1, g])
        pl.when(forwards(g))(lambda: c_f3(g).start())
        c_sib(3, g).start()

    def on_t(g):
        @pl.when(edge)
        def _():
            got(chunk(0, g), rs_h.at[1, g])
            c_t(g).start()

    def on_2(g):
        got(chunk(4, g), rs_h.at[0, g])
        c_sib(2, g).start()

    def on_sib(g):
        for k in range(4):
            got(chunk(2 * k + 1, g), rs_sib.at[k, g])

    def c_lg(d, g):
        return rc(lg_out.at[g, d], lg_in.at[g, d], ss_g.at[0, g], rs_g.at[0, g], at_ctx(ctx + d))

    def c_ls(d, g):
        return rc(ls_out.at[g], ls_in.at[g, d], ss_g.at[1, g], rs_g.at[1, g], at_ctx(ctx - d))

    def c_p(k):
        return rc(pj_in.at[0], pj_in.at[2 * k], ss_o.at[0], rs_o.at[0], at_ctx(ctx - 2 * k))

    def c_ps(k):
        src, to = (pj_in.at[0], 1) if k == 0 else (pj_in.at[2 * k], 2 * k - 1 + 2 * core)
        if k == 4:
            to = 7
        return rc(src, pj_in.at[to], ss_o.at[2], rs_o.at[2], sibling)

    def share_proj():
        got(pj_in.at[pl.ds(1, 4)], rs_o.at[0])
        for k in (1, 2, 3):
            c_ps(k).start()

        @pl.when(core == 0)
        def _():
            c_ps(4).start()

        @pl.when(core == 1)
        def _():
            c_ps(0).start()

    def c_m(d):
        return rc(mp_out.at[d], mp_in.at[d], ss_o.at[1], rs_o.at[1], at_ctx(ctx + d))

    def stage_a(g):
        each(1, REACH + 1, lambda d: c_lg(d, g).start())

    def stage_b(g):
        got(lg_in.at[g, pl.ds(1, REACH)], rs_g.at[0, g])
        logs = [lg_out[g, 0]]
        for d in range(1, REACH + 1):
            logs.append(jnp.where(ctx >= d, lg_in[g, d], LOW))
        top = functools.reduce(jnp.maximum, logs)
        total = functools.reduce(jnp.add, [jnp.exp2(a - top) for a in logs])
        ls_out[g] = top + jnp.log2(total)
        each(1, REACH + 1, lambda d: c_ls(d, g).start())

    def c_rs(k, g):
        r = (rank + k) % 32
        return rc(xp.at[g, r], xr.at[g, rank], ss_g.at[2, g], rs_g.at[2, g], at_rank(r))

    def c_z(k, g):
        return rc(xz.at[g, zz], xz.at[g, zz], ss_g.at[3, g], rs_g.at[3, g], at_z((zz + k) % 8))

    def c_ag(k, g):
        ref = psum.at[g, rank]
        return rc(ref, ref, ss_g.at[4, g], rs_g.at[4, g], at_rank((rank + k) % 32))

    def stage_c(g):
        got(ls_in.at[g, pl.ds(1, REACH)], rs_g.at[1, g])
        lane = lax.broadcasted_iota(jnp.int32, (PER, FR), 1)
        accs = [jnp.zeros((RANK, FR), F32) for _ in range(PER)]
        for d in range(REACH + 1):
            ls = unfold(ls_out[g] if d == 0 else ls_in[g, d])
            pos = (ctx + d) * FR + lane
            f = jnp.exp2(stat(mx, d, g)[...][:PER] - ls)
            f = jnp.where((pos < len_ref[0]) & (ctx + d < 32), f, 0.0)
            stat(fac, d, g)[...] = jnp.concatenate([f, f], axis=0)
            pj = pj_in[d].astype(F32)
            for i in range(PER):
                pf = (pj * f[i : i + 1, :]).astype(BF16)
                accs[i] = accs[i] + nt(pf, ebuf[d * HEADS + g * PER + i])
        for i in range(PER):
            hs = slice((g * PER + i) * HD, (g * PER + i + 1) * HD)
            xp[g, 8 * i : 8 * i + 8] = nn(accs[i].astype(BF16), v_ref[:, hs]).reshape(8, 8, HD)
        each(1, 32, lambda k: c_rs(k, g).start())

    def stage_f(g):
        xr[g, rank] = xp[g, rank]
        got(xr.at[g, pl.ds(0, 31)], rs_g.at[2, g])
        total = xr[g, 0]
        for r in range(1, 32):
            total = total + xr[g, r]
        xz[g, zz] = total
        each(1, 8, lambda k: c_z(k, g).start())

    def stage_g(g):
        got(xz.at[g, pl.ds(0, 7)], rs_g.at[3, g])
        total = xz[g, 0]
        for z in range(1, 8):
            total = total + xz[g, z]
        psum[g, rank] = total
        each(1, 32, lambda k: c_ag(k, g).start())

    def p_head(g, i):
        return psum[g, 8 * i : 8 * i + 8].reshape(RANK, HD)

    def stage_i(g):
        got(psum.at[g, pl.ds(0, 31)], rs_g.at[4, g])
        us = []
        for i in range(PER):
            hs = slice((g * PER + i) * HD, (g * PER + i + 1) * HD)
            us.append(nt(p_head(g, i).astype(BF16), v_ref[:, hs]).astype(BF16))

        def part_of(d, start):
            f = stat(fac, d, g)[...]
            acc = start
            for i in range(PER):
                acc = acc + nn(us[i], ebuf[d * HEADS + g * PER + i]) * f[i : i + 1, :]
            return acc

        for i in range(REACH + 1):
            d = REACH - i
            acc = part_of(d, jnp.zeros((RANK, FR), F32) if g == 0 else yacc[d])
            if g < GROUPS - 1 or d == 0:
                yacc[d] = acc
            else:
                mp_out[d] = acc.astype(BF16)
                c_m(d).start()

    loads[0].wait()
    for g in range(PARTS):
        c_x(g).start()

        @pl.when(core == 1)
        def _():
            c_sib(0, g).start()

    early = PARTS // 2

    def own_down(g):
        pl.when(zh > 0)(lambda: c_dm(g, True).start())

    def own_up(g):
        pl.when(zh == 3)(lambda: c_dp(g, True).start())

    for g in range(PARTS):
        own_down(g)
        if g < early:
            own_up(g)

    def pass_on(g):
        if g < early:
            pl.when(zh == 0)(lambda: c_dm(g, False).start())
        pl.when(zh < 3)(lambda: c_dp(g, False).start())

    def late_down():
        for g in range(early, PARTS):
            pl.when(zh == 0)(lambda: c_dm(g, False).start())

    def late_up():
        for g in range(early, PARTS):
            own_up(g)

    for load in loads[1:4]:
        load.wait()
    pj_in[0] = nt(qi_ref[...], g_ref[...]).astype(BF16)
    each(1, 5, lambda k: c_p(k).start())
    loads[4].wait()
    on_x(0)
    pass_on(0)
    unit(0, 0)
    unit(8, 0)
    on_x(1)
    pass_on(1)
    unit(0, 1)
    unit(8, 1)
    on_1(0)
    on_x(2)
    pass_on(2)
    on_3(0)
    on_x(3)
    pass_on(3)
    on_1(1)
    late_down()
    on_3(1)
    late_up()
    unit(0, 2)
    unit(8, 2)
    unit(0, 3)
    unit(8, 3)
    unit(2, 0)
    unit(6, 0)
    unit(2, 1)
    unit(6, 1)
    on_t(0)
    on_1(2)
    on_3(2)
    unit(2, 2)
    unit(6, 2)
    on_t(1)
    on_1(3)
    on_3(3)
    unit(2, 3)
    unit(6, 3)

    def complete(g):
        on_2(g)
        unit(4, g)
        on_sib(g)
        odd_units(g)
        stage_a(g)

    complete(0)
    share_proj()
    complete(2)
    got(pj_in.at[pl.ds(1, 4)], rs_o.at[2])
    stage_b(0)
    complete(1)
    stage_b(2)
    stage_c(0)
    complete(3)
    stage_b(1)
    stage_c(2)
    stage_b(3)
    stage_c(1)
    stage_f(0)
    stage_f(2)
    stage_c(3)
    stage_f(1)
    stage_g(0)
    stage_g(2)
    stage_f(3)
    stage_g(1)
    stage_g(3)
    stage_i(0)
    stage_i(1)
    stage_i(2)
    stage_i(3)

    p_sum = jnp.concatenate([p_head(g, i) for g in range(GROUPS) for i in range(PER)], axis=1)
    gram = nt(p_sum, p_sum, precision=lax.Precision.HIGHEST)
    row_i = lax.broadcasted_iota(jnp.int32, (RANK, 2 * RANK), 0)
    col_i = lax.broadcasted_iota(jnp.int32, (RANK, 2 * RANK), 1)
    a = jnp.concatenate([gram, jnp.zeros((RANK, RANK), F32)], axis=1)
    a = jnp.where(col_i == row_i + RANK, 1.0, a)
    pivots = jnp.zeros((RANK, 2 * RANK), F32)
    for k in range(RANK):
        wide = jnp.broadcast_to(a[:, k : k + 1], (RANK, 2 * RANK))
        piv = wide[k : k + 1, :]
        line = a[k : k + 1, :] / piv
        pivots = jnp.where(row_i == k, piv, pivots)
        a = a - jnp.where(row_i > k, wide, 0.0) * line
    inv_low = a[:, RANK:] * (lax.rsqrt(pivots[:, RANK:]) * (WIDTH**0.5))

    got(mp_in.at[pl.ds(1, REACH)], rs_o.at[1])
    acc = yacc[0]
    for d in range(1, REACH + 1):
        acc = acc + jnp.where(ctx >= d, mp_in[d].astype(F32), 0.0)
    mapped = nn(inv_low, acc, precision=lax.Precision.HIGHEST).astype(BF16)

    half_w = D // 2
    mine = pl.ds(pl.multiple_of(core * half_w, half_w), half_w)
    other = pl.ds(pl.multiple_of((1 - core) * half_w, half_w), half_w)
    step = 512

    def q_cols(base, i):
        s = pl.ds(pl.multiple_of(base + i * step, step), step)
        xq[:, s] = nn(mapped, g_ref[:, s])

    each(0, half_w // step, lambda i: q_cols((1 - core) * half_w, i))
    cc = rc(xq.at[:, other], xq_c, ss_q.at[0], rs_q.at[0], sibling)
    cc.start()
    each(0, half_w // step, lambda i: q_cols(core * half_w, i))
    cc.wait_recv()

    def join(i):
        s = pl.ds(pl.multiple_of(i * 128, 128), 128)
        t = pl.ds(pl.multiple_of(core * half_w + i * 128, 128), 128)
        xq_b[i] = (xq_c[:, s] + xq[:, t]).astype(BF16)

    each(0, 16, join)

    def c_qx(k):
        p = (plane + k) % 16
        return rc(xq_b.at[p], xq_xy.at[plane], ss_q.at[1], rs_q.at[1], at_plane(p))

    each(1, 16, lambda k: c_qx(k).start())
    xq_xy[plane] = xq_b[plane]
    got(xq_xy.at[pl.ds(0, 15)], rs_q.at[1])
    total = xq_xy[0].astype(F32)
    for p in range(1, 16):
        total = total + xq_xy[p].astype(F32)
    xq_z[zz] = total.astype(BF16)

    def c_qz(k):
        return rc(xq_z.at[zz], xq_z.at[zz], ss_q.at[2], rs_q.at[2], at_z((zz + k) % 8))

    each(1, 8, lambda k: c_qz(k).start())
    phat_ref[...] = nn(inv_low, p_sum, precision=lax.Precision.HIGHEST)
    got(xq_z.at[pl.ds(0, 7)], rs_q.at[2])
    total = xq_z[0].astype(F32)
    for z in range(1, 8):
        total = total + xq_z[z].astype(F32)
    done = total * (1.0 / 256.0)
    qg[core, plane] = done.astype(BF16)

    def c_qa(k):
        ref = qg.at[core, plane]
        return rc(ref, ref, ss_q.at[3], rs_q.at[3], at_plane((plane + k) % 16))

    each(1, 16, lambda k: c_qa(k).start())
    got(qg.at[core, pl.ds(0, 15)], rs_q.at[3])
    c2 = rc(qg.at[core], qg.at[core], ss_q.at[4], rs_q.at[4], sibling)
    c2.start()
    got(qg.at[1 - core], rs_q.at[4])
    for i in range(32):
        qnew_ref[:, i * 128 : i * 128 + 128] = qg[i // 16, i % 16].astype(F32)

    for g in range(PARTS):
        c_x(g).wait_send()
        c_dm(g, True).wait_send()
        c_dp(g, True).wait_send()

        @pl.when(forwards(g))
        def _():
            c_f1(g).wait_send()
            c_f3(g).wait_send()

        for k in (1, 2, 3):
            c_sib(k, g).wait_send()

        if g < PARTS // 2:

            @pl.when(edge)
            def _():
                c_t(g).wait_send()

        @pl.when(core == 1)
        def _():
            c_sib(0, g).wait_send()

        @pl.when(core == 0)
        def _():
            c_sib(4, g).wait_send()

    for g in range(GROUPS):
        left_all(lg_in.at[g, pl.ds(0, REACH)], ss_g.at[0, g])
        left_all(ls_in.at[g, pl.ds(0, REACH)], ss_g.at[1, g])
        left_all(xr.at[g, pl.ds(0, 31)], ss_g.at[2, g])
        left_all(xz.at[g, pl.ds(0, 7)], ss_g.at[3, g])
        left_all(psum.at[g, pl.ds(0, 31)], ss_g.at[4, g])
    left_all(pj_in.at[pl.ds(0, 4)], ss_o.at[0])
    left_all(pj_in.at[pl.ds(0, 4)], ss_o.at[2])
    left_all(mp_in.at[pl.ds(0, REACH)], ss_o.at[1])
    cc.wait_send()
    left_all(xq_xy.at[pl.ds(0, 15)], ss_q.at[1])
    left_all(xq_z.at[pl.ds(0, 7)], ss_q.at[2])
    left_all(qg.at[core, pl.ds(0, 15)], ss_q.at[3])
    c2.wait_send()


def local(queries, keys, values, out_grad, q_init, lengths):
    dma = pltpu.SemaphoreType.DMA
    n = REACH + 1
    vm = pl.BlockSpec(memory_space=pltpu.VMEM)
    p_hat, q_new = pl.pallas_call(
        kernel,
        out_shape=(
            jax.ShapeDtypeStruct((RANK, WIDTH), F32),
            jax.ShapeDtypeStruct((RANK, D), F32),
        ),
        in_specs=[pl.BlockSpec(memory_space=pltpu.SMEM)] + [pl.BlockSpec(memory_space=pl.ANY)] * 5,
        out_specs=(vm, vm),
        scratch_shapes=[
            pltpu.VMEM((FR, WIDTH), BF16),
            pltpu.VMEM((FR, WIDTH), BF16),
            pltpu.VMEM((FR, WIDTH), BF16),
            pltpu.VMEM((FR, D), BF16),
            pltpu.VMEM((RANK, D), BF16),
            pltpu.VMEM((n, FR, WIDTH), BF16),
            pltpu.VMEM((n * HEADS, FR, FR), BF16),
            pltpu.VMEM((n * GROUPS * 8, FR), F32),
            pltpu.VMEM((GROUPS, n, 8, 128), F32),
            pltpu.VMEM((GROUPS, n, 8, 128), F32),
            pltpu.VMEM((GROUPS, 8, 128), F32),
            pltpu.VMEM((GROUPS, n, 8, 128), F32),
            pltpu.VMEM((n * GROUPS * 8, FR), F32),
            pltpu.VMEM((n, RANK, FR), BF16),
            pltpu.VMEM((n, RANK, FR), F32),
            pltpu.VMEM((n, RANK, FR), BF16),
            pltpu.VMEM((n, RANK, FR), BF16),
            pltpu.VMEM((GROUPS, 32, 8, 128), F32),
            pltpu.VMEM((GROUPS, 32, 8, 128), F32),
            pltpu.VMEM((GROUPS, 8, 8, 128), F32),
            pltpu.VMEM((GROUPS, 32, 8, 128), F32),
            pltpu.VMEM((RANK, D), F32),
            pltpu.VMEM((RANK, D // 2), F32),
            pltpu.VMEM((16, RANK, 128), BF16),
            pltpu.VMEM((16, RANK, 128), BF16),
            pltpu.VMEM((8, RANK, 128), BF16),
            pltpu.VMEM((2, 16, RANK, 128), BF16),
            dma((5,)), dma((4,)), dma((4,)), dma((4,)), dma((4,)), dma((4,)), dma((4,)), dma((5, 4)),
            dma((3, 4)), dma((2, 4)), dma((4, 4)),
            dma((5, GROUPS)), dma((5, GROUPS)), dma((3,)), dma((3,)), dma((5,)), dma((5,)),
        ],
        compiler_params=pltpu.CompilerParams(
            collective_id=0, has_side_effects=True, vmem_limit_bytes=60 << 20
        ),
        name="attend",
    )(lengths, queries[0], keys[0], values[0], out_grad[0], q_init)
    return (p_hat, q_new)


def solution(mesh):
    placed = (
        P("dp", "ctx", None),
        P("dp", "ctx", None),
        P("dp", "ctx", None),
        P("dp", "ctx", None),
        P(),
        P("dp"),
    )
    return jax.shard_map(local, mesh=mesh, in_specs=placed, out_specs=(P(), P()), check_vma=False)
```

time: 1020 us -> 182 us (0.18)
  waiting for transfers between devices: 744 us -> 0 us
  Pallas kernels: 0 us -> 176 us
  starting transfers between devices: 166 us -> 0 us
  matrix products: 37.3 us -> 0 us
  other arithmetic: 26.4 us -> 0 us
  local copies, waits for them, and re-layouts: 26.1 us -> 4.14 us
  between operations: 15.4 us -> 1.29 us
    psum x2 -> x0, waiting for transfers between devices: 506 us -> none  [the longest x1 255 us: local(): q_new = lax.psum(q_term, ('dp', 'ctx')) / all_frames ** 0.5]
    ppermute x8 -> x0, waiting for transfers between devices: 239 us -> none  [passed_along(): return lax.ppermute(block, axis, route)]
    pallas_call x0 -> x1, Pallas kernels: none -> 176 us  [local(): pl.pallas_call(kernel, out_shape=(jax.ShapeDtypeStruct((RANK, WIDTH), F32...]
    ppermute x8 -> x0, starting transfers between devices: 165 us -> none  [passed_along(): return lax.ppermute(block, axis, route)]
    dot_general x21 -> x0, matrix products: 34.8 us -> none  [the longest x9 15.7 us: absorb(): jnp.einsum('hqk,khe->qhe', expo.astype(jnp.bfloat16), v_heads, preferred_...]
    slice x8 -> x0, local copies, waits for them, and re-layouts: 17.7 us -> none  [the longest x7 14.7 us: absorb(): v_heads = piece[1].reshape(frames, heads, HEAD_DIM)]
    another operation x6 -> x0, other arithmetic: 14.8 us -> none  [the longest x3 6.52 us: local(): lower = jnp.linalg.cholesky(gram)]
  transfers between devices with their start and end apart: 10 -> 0, of which waited for: 6 -> 0; matrix products, arithmetic and copies ran while one was open for 3% -> 0% of each run, Pallas kernels for 0% -> 0%
where the time goes in v2:
time: 182 us; the launch traced here: 181 us
  Pallas kernels  176 us (97%)
  local copies, waits for them, and re-layouts  4.14 us (2%)
    pallas_call x1, Pallas kernels, local(): pl.pallas_call(kernel, out_shape=(jax.ShapeDtypeStruct((RANK, WIDTH), F32...  176 us
    unnamed x2, local copies, waits for them, and re-layouts  4.14 us

profile of v2, /device:TPU:1, one launch (start us, length us, event | category | flops | bytes accessed | tf_op | source)
XLA Modules:
  0.0 181.5 jit_solution(12566064343605920614)
XLA Ops:
  1.3 176.1 %attend.1 = (f32[64,2048]{1,0:T(8,128)}, f32[64,4096]{1,0:T(8,128)}) custom-call(s32[1]{0:T(128)S(6)} %copy.10.len_ref, bf16[256,2048]{1,0:T(8,128)(2,1)} %bitcast.5, bf16[256,2048]{1,0:T(8,128)(2,1)} %bitcast.6, bf16[256,2048]{1,0:T(8,128)(2,1)} %bitcast.7, bf16[256,4096]{1,0:T(8,128)(2,1)} %bitcast.4, bf16[64,4096]{1,0:T(8,128)(2,1)} %qi_any.1), custom_call_target="tpu_custom_call" | custom-call | tf_op jit(solution)/shard_map/attend/pallas_call | solution.py:575
  177.3 1.9 %copy.11 = f32[64,2048]{1,0:T(8,128)} copy(f32[64,2048]{1,0:T(8,128)} %get-tuple-element.4) | data formatting | bytes 1048576
  179.2 2.3 %copy.12 = f32[64,4096]{1,0:T(8,128)} copy(f32[64,4096]{1,0:T(8,128)} %get-tuple-element.5) | data formatting | bytes 2097152

commit v3 on v2

--- a/solution.py
+++ b/solution.py
@@ -113,6 +113,23 @@
 
     def c_x(g):
         return rc(q_ref.at[:, cols(g)], chunk(8, g), ss_x.at[g], rs_slot.at[2, g], left)
+
+    def sub(ref, p):
+        return ref.at[:, pl.ds(p * CH // 2, CH // 2)]
+
+    def c_x0(p):
+        return rc(sub(q_ref, p), sub(qbuf.at[8], p), ss_x.at[4 * p], rs_slot.at[2, 4 * p], left)
+
+    def pass_half(p):
+        src = sub(qbuf.at[8], p)
+
+        @pl.when(zh == 0)
+        def _():
+            rc(src, sub(qbuf.at[2], p), ss_dm.at[0], rs_slot.at[0, 0], down).start()
+
+        @pl.when(zh < 3)
+        def _():
+            rc(src, sub(qbuf.at[6], p), ss_dp.at[0], rs_slot.at[1, 0], up).start()
 
     def c_dm(g, own):
         src = q_ref.at[:, cols(g)] if own else chunk(8, g)
@@ -185,11 +202,20 @@
         stat(mx, d, g)[...] = jnp.concatenate([top, top], axis=0)
         lg_out[g, d] = fold(logs)
 
-    def odd_units(g):
-        each(0, 4, lambda i: unit(1 + 2 * i, g))
+    def early_odd(g):
+        for k in (0, 3, 1 + core):
+            on_sib(g, k)
+        unit(1, g)
+        unit(7, g)
+        unit(3 + 2 * core, g)
 
     def on_x(g):
-        got(chunk(8, g), rs_slot.at[2, g])
+        if g == 0:
+            for p in range(2):
+                got(sub(qbuf.at[8], p), rs_slot.at[2, 4 * p])
+                pass_half(p)
+        else:
+            got(chunk(8, g), rs_slot.at[2, g])
 
         @pl.when(core == 0)
         def _():
@@ -215,9 +241,8 @@
         got(chunk(4, g), rs_h.at[0, g])
         c_sib(2, g).start()
 
-    def on_sib(g):
-        for k in range(4):
-            got(chunk(2 * k + 1, g), rs_sib.at[k, g])
+    def on_sib(g, k):
+        got(chunk(2 * k + 1, g), rs_sib.at[k, g])
 
     def c_lg(d, g):
         return rc(lg_out.at[g, d], lg_in.at[g, d], ss_g.at[0, g], rs_g.at[0, g], at_ctx(ctx + d))
@@ -338,7 +363,11 @@
 
     loads[0].wait()
     for g in range(PARTS):
-        c_x(g).start()
+        if g == 0:
+            c_x0(0).start()
+            c_x0(1).start()
+        else:
+            c_x(g).start()
 
         @pl.when(core == 1)
         def _():
@@ -376,7 +405,6 @@
     each(1, 5, lambda k: c_p(k).start())
     loads[4].wait()
     on_x(0)
-    pass_on(0)
     unit(0, 0)
     unit(8, 0)
     on_x(1)
@@ -399,46 +427,50 @@
     unit(8, 3)
     unit(2, 0)
     unit(6, 0)
+    early_odd(0)
     unit(2, 1)
     unit(6, 1)
     on_t(0)
+    early_odd(1)
     on_1(2)
     on_3(2)
     unit(2, 2)
     unit(6, 2)
     on_t(1)
+    early_odd(2)
     on_1(3)
     on_3(3)
     unit(2, 3)
     unit(6, 3)
+    early_odd(3)
 
     def complete(g):
         on_2(g)
         unit(4, g)
-        on_sib(g)
-        odd_units(g)
+        on_sib(g, 2 - core)
+        unit(5 - 2 * core, g)
         stage_a(g)
 
     complete(0)
     share_proj()
     complete(2)
+    complete(1)
     got(pj_in.at[pl.ds(1, 4)], rs_o.at[2])
     stage_b(0)
-    complete(1)
+    complete(3)
     stage_b(2)
+    stage_b(1)
     stage_c(0)
-    complete(3)
-    stage_b(1)
+    stage_b(3)
     stage_c(2)
-    stage_b(3)
     stage_c(1)
+    stage_c(3)
     stage_f(0)
     stage_f(2)
-    stage_c(3)
     stage_f(1)
+    stage_f(3)
     stage_g(0)
     stage_g(2)
-    stage_f(3)
     stage_g(1)
     stage_g(3)
     stage_i(0)
@@ -526,7 +558,11 @@
         qnew_ref[:, i * 128 : i * 128 + 128] = qg[i // 16, i % 16].astype(F32)
 
     for g in range(PARTS):
-        c_x(g).wait_send()
+        if g == 0:
+            c_x0(0).wait_send()
+            c_x0(1).wait_send()
+        else:
+            c_x(g).wait_send()
         c_dm(g, True).wait_send()
         c_dp(g, True).wait_send()
 
@@ -568,11 +604,16 @@
     c2.wait_send()
 
 
+def hand_over(p_in, q_in, p_out, q_out):
+    p_out[...] = p_in[...]
+    q_out[...] = q_in[...]
+
+
 def local(queries, keys, values, out_grad, q_init, lengths):
     dma = pltpu.SemaphoreType.DMA
     n = REACH + 1
     vm = pl.BlockSpec(memory_space=pltpu.VMEM)
-    p_hat, q_new = pl.pallas_call(
+    outs = pl.pallas_call(
         kernel,
         out_shape=(
             jax.ShapeDtypeStruct((RANK, WIDTH), F32),
@@ -608,8 +649,8 @@
             pltpu.VMEM((16, RANK, 128), BF16),
             pltpu.VMEM((8, RANK, 128), BF16),
             pltpu.VMEM((2, 16, RANK, 128), BF16),
-            dma((5,)), dma((4,)), dma((4,)), dma((4,)), dma((4,)), dma((4,)), dma((4,)), dma((5, 4)),
-            dma((3, 4)), dma((2, 4)), dma((4, 4)),
+            dma((5,)), dma((5,)), dma((4,)), dma((4,)), dma((4,)), dma((4,)), dma((4,)), dma((5, 4)),
+            dma((3, 5)), dma((2, 4)), dma((4, 4)),
             dma((5, GROUPS)), dma((5, GROUPS)), dma((3,)), dma((3,)), dma((5,)), dma((5,)),
         ],
         compiler_params=pltpu.CompilerParams(
@@ -617,7 +658,13 @@
         ),
         name="attend",
     )(lengths, queries[0], keys[0], values[0], out_grad[0], q_init)
-    return (p_hat, q_new)
+    return pl.pallas_call(
+        hand_over,
+        out_shape=tuple(jax.ShapeDtypeStruct(o.shape, F32) for o in outs),
+        in_specs=[vm] * 2,
+        out_specs=(vm,) * 2,
+        name="hand_over",
+    )(*outs)
 
 
 def solution(mesh):

time: 182 us -> 168 us (0.923)
  Pallas kernels: 176 us -> 167 us
  local copies, waits for them, and re-layouts: 4.14 us -> 0 us
    pallas_call x1, Pallas kernels: 176 us -> 164 us  [local(): pl.pallas_call(kernel, out_shape=(jax.ShapeDtypeStruct((RANK, WIDTH), F32...]
    unnamed x2 -> x0, local copies, waits for them, and re-layouts: 4.14 us -> none
    pallas_call x0 -> x1, Pallas kernels: none -> 2.57 us  [local(): pl.pallas_call(hand_over, out_shape=tuple((jax.ShapeDtypeStruct(o.shape,...]
where the time goes in v3:
time: 168 us
  Pallas kernels  167 us (99%)
    pallas_call x1, Pallas kernels, local(): pl.pallas_call(kernel, out_shape=(jax.ShapeDtypeStruct((RANK, WIDTH), F32...  164 us

profile of v3, /device:TPU:1, one launch (start us, length us, event | category | flops | bytes accessed | tf_op | source)
XLA Modules:
  0.0 168.1 jit_solution(13787938560592031659)
XLA Ops:
  1.3 164.2 %attend.1 = (f32[64,2048]{1,0:T(8,128)}, f32[64,4096]{1,0:T(8,128)}) custom-call(s32[1]{0:T(128)S(6)} %copy.8.len_ref, bf16[256,2048]{1,0:T(8,128)(2,1)} %bitcast.5, bf16[256,2048]{1,0:T(8,128)(2,1)} %bitcast.6, bf16[256,2048]{1,0:T(8,128)(2,1)} %bitcast.7, bf16[256,4096]{1,0:T(8,128)(2,1)} %bitcast.4, bf16[64,4096]{1,0:T(8,128)(2,1)} %qi_any.1), custom_call_target="tpu_custom_call" | custom-call | tf_op jit(solution)/shard_map/attend/pallas_call | solution.py:616
  165.5 2.6 %hand_over.1 = (f32[64,2048]{1,0:T(8,128)}, f32[64,4096]{1,0:T(8,128)}) custom-call(f32[64,2048]{1,0:T(8,128)} %get-tuple-element.4.p_in, f32[64,4096]{1,0:T(8,128)} %get-tuple-element.5.q_in), custom_call_target="tpu_custom_call" | custom-call | tf_op jit(solution)/shard_map/hand_over/pallas_call | solution.py:661

commit v4 on v3

--- a/solution.py
+++ b/solution.py
@@ -115,12 +115,13 @@
         return rc(q_ref.at[:, cols(g)], chunk(8, g), ss_x.at[g], rs_slot.at[2, g], left)
 
     def sub(ref, p):
-        return ref.at[:, pl.ds(p * CH // 2, CH // 2)]
+        return ref.at[:, pl.ds(p * CH // 4, CH // 4)]
 
     def c_x0(p):
-        return rc(sub(q_ref, p), sub(qbuf.at[8], p), ss_x.at[4 * p], rs_slot.at[2, 4 * p], left)
-
-    def pass_half(p):
+        i = 0 if p == 0 else 3 + p
+        return rc(sub(q_ref, p), sub(qbuf.at[8], p), ss_x.at[i], rs_slot.at[2, i], left)
+
+    def pass_piece(p):
         src = sub(qbuf.at[8], p)
 
         @pl.when(zh == 0)
@@ -211,9 +212,9 @@
 
     def on_x(g):
         if g == 0:
-            for p in range(2):
-                got(sub(qbuf.at[8], p), rs_slot.at[2, 4 * p])
-                pass_half(p)
+            for p in range(4):
+                got(sub(qbuf.at[8], p), rs_slot.at[2, 0 if p == 0 else 3 + p])
+                pass_piece(p)
         else:
             got(chunk(8, g), rs_slot.at[2, g])
 
@@ -364,8 +365,8 @@
     loads[0].wait()
     for g in range(PARTS):
         if g == 0:
-            c_x0(0).start()
-            c_x0(1).start()
+            for p in range(4):
+                c_x0(p).start()
         else:
             c_x(g).start()
 
@@ -405,16 +406,16 @@
     each(1, 5, lambda k: c_p(k).start())
     loads[4].wait()
     on_x(0)
+    on_x(1)
+    pass_on(1)
     unit(0, 0)
     unit(8, 0)
-    on_x(1)
-    pass_on(1)
-    unit(0, 1)
-    unit(8, 1)
     on_1(0)
     on_x(2)
     pass_on(2)
     on_3(0)
+    unit(0, 1)
+    unit(8, 1)
     on_x(3)
     pass_on(3)
     on_1(1)
@@ -428,15 +429,15 @@
     unit(2, 0)
     unit(6, 0)
     early_odd(0)
+    on_t(0)
     unit(2, 1)
     unit(6, 1)
-    on_t(0)
     early_odd(1)
     on_1(2)
     on_3(2)
+    on_t(1)
     unit(2, 2)
     unit(6, 2)
-    on_t(1)
     early_odd(2)
     on_1(3)
     on_3(3)
@@ -519,13 +520,16 @@
         t = pl.ds(pl.multiple_of(core * half_w + i * 128, 128), 128)
         xq_b[i] = (xq_c[:, s] + xq[:, t]).astype(BF16)
 
-    each(0, 16, join)
-
     def c_qx(k):
         p = (plane + k) % 16
         return rc(xq_b.at[p], xq_xy.at[plane], ss_q.at[1], rs_q.at[1], at_plane(p))
 
-    each(1, 16, lambda k: c_qx(k).start())
+    def join_send(k):
+        join((plane + k) % 16)
+        c_qx(k).start()
+
+    each(1, 16, join_send)
+    join(plane)
     xq_xy[plane] = xq_b[plane]
     got(xq_xy.at[pl.ds(0, 15)], rs_q.at[1])
     total = xq_xy[0].astype(F32)
@@ -553,14 +557,17 @@
     got(qg.at[core, pl.ds(0, 15)], rs_q.at[3])
     c2 = rc(qg.at[core], qg.at[core], ss_q.at[4], rs_q.at[4], sibling)
     c2.start()
-    got(qg.at[1 - core], rs_q.at[4])
-    for i in range(32):
-        qnew_ref[:, i * 128 : i * 128 + 128] = qg[i // 16, i % 16].astype(F32)
+    for j in (core, 1 - core):
+        if j is not core:
+            got(qg.at[j], rs_q.at[4])
+        for i in range(16):
+            s = pl.ds(pl.multiple_of(j * half_w + i * 128, 128), 128)
+            qnew_ref[:, s] = qg[j, i].astype(F32)
 
     for g in range(PARTS):
         if g == 0:
-            c_x0(0).wait_send()
-            c_x0(1).wait_send()
+            for p in range(4):
+                c_x0(p).wait_send()
         else:
             c_x(g).wait_send()
         c_dm(g, True).wait_send()
@@ -649,8 +656,8 @@
             pltpu.VMEM((16, RANK, 128), BF16),
             pltpu.VMEM((8, RANK, 128), BF16),
             pltpu.VMEM((2, 16, RANK, 128), BF16),
-            dma((5,)), dma((5,)), dma((4,)), dma((4,)), dma((4,)), dma((4,)), dma((4,)), dma((5, 4)),
-            dma((3, 5)), dma((2, 4)), dma((4, 4)),
+            dma((5,)), dma((7,)), dma((4,)), dma((4,)), dma((4,)), dma((4,)), dma((4,)), dma((5, 4)),
+            dma((3, 7)), dma((2, 4)), dma((4, 4)),
             dma((5, GROUPS)), dma((5, GROUPS)), dma((3,)), dma((3,)), dma((5,)), dma((5,)),
         ],
         compiler_params=pltpu.CompilerParams(

time: 168 us -> 167 us (level)
  Pallas kernels: 167 us -> 165 us
where the time goes in v4:
time: 167 us; the launch traced here: 166 us
  Pallas kernels  165 us (99%)
    pallas_call x1, Pallas kernels, local(): pl.pallas_call(kernel, out_shape=(jax.ShapeDtypeStruct((RANK, WIDTH), F32...  163 us

profile of v4, /device:TPU:1, one launch (start us, length us, event | category | flops | bytes accessed | tf_op | source)
XLA Modules:
  0.0 166.5 jit_solution(3334971843369946803)
XLA Ops:
  1.3 162.6 %attend.1 = (f32[64,2048]{1,0:T(8,128)}, f32[64,4096]{1,0:T(8,128)}) custom-call(s32[1]{0:T(128)S(6)} %copy.8.len_ref, bf16[256,2048]{1,0:T(8,128)(2,1)} %bitcast.5, bf16[256,2048]{1,0:T(8,128)(2,1)} %bitcast.6, bf16[256,2048]{1,0:T(8,128)(2,1)} %bitcast.7, bf16[256,4096]{1,0:T(8,128)(2,1)} %bitcast.4, bf16[64,4096]{1,0:T(8,128)(2,1)} %qi_any.1), custom_call_target="tpu_custom_call" | custom-call | tf_op jit(solution)/shard_map/attend/pallas_call | solution.py:623
  163.9 2.6 %hand_over.1 = (f32[64,2048]{1,0:T(8,128)}, f32[64,4096]{1,0:T(8,128)}) custom-call(f32[64,2048]{1,0:T(8,128)} %get-tuple-element.4.p_in, f32[64,4096]{1,0:T(8,128)} %get-tuple-element.5.q_in), custom_call_target="tpu_custom_call" | custom-call | tf_op jit(solution)/shard_map/hand_over/pallas_call | solution.py:668

commit v5 on v4

--- a/solution.py
+++ b/solution.py
@@ -502,18 +502,25 @@
 
     half_w = D // 2
     mine = pl.ds(pl.multiple_of(core * half_w, half_w), half_w)
-    other = pl.ds(pl.multiple_of((1 - core) * half_w, half_w), half_w)
     step = 512
 
     def q_cols(base, i):
         s = pl.ds(pl.multiple_of(base + i * step, step), step)
         xq[:, s] = nn(mapped, g_ref[:, s])
 
-    each(0, half_w // step, lambda i: q_cols((1 - core) * half_w, i))
-    cc = rc(xq.at[:, other], xq_c, ss_q.at[0], rs_q.at[0], sibling)
-    cc.start()
+    quarter = half_w // 2
+
+    def c_cc(p):
+        src = pl.ds(pl.multiple_of((1 - core) * half_w + p * quarter, quarter), quarter)
+        dst = xq_c.at[:, pl.ds(p * quarter, quarter)]
+        return rc(xq.at[:, src], dst, ss_q.at[5 * p], rs_q.at[5 * p], sibling)
+
+    for p in range(2):
+        each(2 * p, 2 * p + 2, lambda i: q_cols((1 - core) * half_w, i))
+        c_cc(p).start()
     each(0, half_w // step, lambda i: q_cols(core * half_w, i))
-    cc.wait_recv()
+    for p in range(2):
+        c_cc(p).wait_recv()
 
     def join(i):
         s = pl.ds(pl.multiple_of(i * 128, 128), 128)
@@ -604,7 +611,8 @@
     left_all(pj_in.at[pl.ds(0, 4)], ss_o.at[0])
     left_all(pj_in.at[pl.ds(0, 4)], ss_o.at[2])
     left_all(mp_in.at[pl.ds(0, REACH)], ss_o.at[1])
-    cc.wait_send()
+    for p in range(2):
+        c_cc(p).wait_send()
     left_all(xq_xy.at[pl.ds(0, 15)], ss_q.at[1])
     left_all(xq_z.at[pl.ds(0, 7)], ss_q.at[2])
     left_all(qg.at[core, pl.ds(0, 15)], ss_q.at[3])
@@ -658,7 +666,7 @@
             pltpu.VMEM((2, 16, RANK, 128), BF16),
             dma((5,)), dma((7,)), dma((4,)), dma((4,)), dma((4,)), dma((4,)), dma((4,)), dma((5, 4)),
             dma((3, 7)), dma((2, 4)), dma((4, 4)),
-            dma((5, GROUPS)), dma((5, GROUPS)), dma((3,)), dma((3,)), dma((5,)), dma((5,)),
+            dma((5, GROUPS)), dma((5, GROUPS)), dma((3,)), dma((3,)), dma((6,)), dma((6,)),
         ],
         compiler_params=pltpu.CompilerParams(
             collective_id=0, has_side_effects=True, vmem_limit_bytes=60 << 20

time: 167 us -> 166 us (level)
  no operation moved by 1% of the time
where the time goes in v5:
time: 166 us
  Pallas kernels  165 us (99%)
    pallas_call x1, Pallas kernels, local(): pl.pallas_call(kernel, out_shape=(jax.ShapeDtypeStruct((RANK, WIDTH), F32...  163 us

profile of v5, /device:TPU:1, one launch (start us, length us, event | category | flops | bytes accessed | tf_op | source)
XLA Modules:
  0.0 166.4 jit_solution(10503340538798777612)
XLA Ops:
  1.3 162.5 %attend.1 = (f32[64,2048]{1,0:T(8,128)}, f32[64,4096]{1,0:T(8,128)}) custom-call(s32[1]{0:T(128)S(6)} %copy.8.len_ref, bf16[256,2048]{1,0:T(8,128)(2,1)} %bitcast.5, bf16[256,2048]{1,0:T(8,128)(2,1)} %bitcast.6, bf16[256,2048]{1,0:T(8,128)(2,1)} %bitcast.7, bf16[256,4096]{1,0:T(8,128)(2,1)} %bitcast.4, bf16[64,4096]{1,0:T(8,128)(2,1)} %qi_any.1), custom_call_target="tpu_custom_call" | custom-call | tf_op jit(solution)/shard_map/attend/pallas_call | solution.py:631
  163.8 2.6 %hand_over.1 = (f32[64,2048]{1,0:T(8,128)}, f32[64,4096]{1,0:T(8,128)}) custom-call(f32[64,2048]{1,0:T(8,128)} %get-tuple-element.4.p_in, f32[64,4096]{1,0:T(8,128)} %get-tuple-element.5.q_in), custom_call_target="tpu_custom_call" | custom-call | tf_op jit(solution)/shard_map/hand_over/pallas_call | solution.py:676
